TPU v7x, 768 devices: a whole 4x8x12 slice. The times are simulated.
768 devices in a mesh: slab: 48 (over z, x), tile: 16 (over y, core).
Axes of the slice: x: 4, y: 8, z: 12, core: 2. Of those that a mesh axis runs over, the one named last changes fastest.
Arguments:
- tiles: bfloat16 [768, 20, 256, 128], P(('slab', 'tile')), may hold values from -6 to 6
- offsets: int32 [768, 2], replicated, may hold values from -3 to 3450, as said below
- fracs: int32 [768, 3], replicated, may hold values from 0 to 15
Outputs:
- joined: bfloat16 [768, 3706, 128], P(('slab', 'tile'))
Inputs may be any that keep to these rules, and one draw needn't show every extreme that they name: offsets[g, 0] lies within 1 of (g // 16) * 16 - 2, and offsets[g, 1] within 4 of (g % 16) * 230, clipped to 0 .. 3450; some tile reaches each end of the plane shift.
All inputs are finite; a program needn't handle non-finite values.
Results may differ from a plain program's by a relative error of at most 0.0038.
Values may be sent and summed in bfloat16 or wider, within the bound.
No kernel may reach another device: no remote copies, remote signals or barrier semaphores. Data moves between devices by JAX's collectives and lax.ppermute only.
A program may use at most 32 MiB of HBM per device.

v0:
```python
import jax
import jax.numpy as jnp
from jax import lax
from jax.sharding import PartitionSpec as P

GROUPZ = 16
MARGIN = 2
JIT = 1
STEPY = 230
RY = 26
RX = 16
QUANT = 16


weight_floor = 0.05


def shifted_2(block, axis, distance):
    devices = range(lax.axis_size(axis))
    route = [(i - distance, i) for i in devices if i - distance in devices]
    return lax.ppermute(block, axis, route)


def rising_at(position, ramp_width):
    rising = 0.5 - 0.5 * jnp.cos(jnp.pi * (position + 1.0) / (ramp_width + 1.0))
    return jnp.where(position < ramp_width, rising, jnp.ones_like(rising))


def ramp_at(index_grid, length, ramp_width):
    position = index_grid.astype(jnp.float32)
    mirrored = (length - 1 - index_grid).astype(jnp.float32)
    return jnp.minimum(rising_at(position, ramp_width), rising_at(mirrored, ramp_width))


def ramp(length, ramp_width):
    return ramp_at(jnp.arange(length, dtype=jnp.int32), length, ramp_width)


def resample(raw_tile, fraction_row):
    volume_field = raw_tile.astype(jnp.float32)
    for direction in range(3):
        fraction = fraction_row[direction].astype(jnp.float32) / QUANT
        extent = volume_field.shape[direction]
        shifted = jnp.concatenate(
            [
                lax.slice_in_dim(volume_field, 1, extent, axis=direction),
                jnp.zeros_like(lax.slice_in_dim(volume_field, 0, 1, axis=direction)),
            ],
            axis=direction,
        )
        volume_field = (1.0 - fraction) * volume_field + fraction * shifted
    return volume_field


def lookup_rows(offsets, tile_ids):
    grid = jnp.arange(offsets.shape[0], dtype=jnp.int32)
    hits = tile_ids[:, None] == grid[None, :]
    return jnp.sum(
        jnp.where(hits[:, :, None], offsets[None, :, :], jnp.zeros_like(offsets)[None, :, :]),
        axis=1,
    )


def take_planes(source, positions, usable):
    planes = jnp.take(source, jnp.clip(positions, 0, source.shape[0] - 1), axis=0)
    return jnp.where(usable[:, :, None, None], planes, jnp.zeros_like(planes))


def shards(tiles, offsets, fracs):
    group_size = lax.axis_size("tile")
    group_total = lax.axis_size("slab")
    slab_index = lax.axis_index("slab")
    owner_index = lax.axis_index("tile")
    depth = tiles.shape[1]
    tile_rows = tiles.shape[2]
    columns = tiles.shape[3]
    per_slab = GROUPZ // group_size
    tile_total = offsets.shape[0]
    self_id = slab_index * group_size + owner_index
    fraction_row = lax.dynamic_index_in_dim(fracs, self_id, 0, keepdims=False)
    corner = lax.dynamic_index_in_dim(offsets, self_id, 0, keepdims=False)
    ramp_z = ramp(depth, 2 * MARGIN)
    ramp_y = ramp(tile_rows, RY)
    ramp_x = ramp(columns, RX)
    weight = ramp_z[:, None, None] * ramp_y[None, :, None] * ramp_x[None, None, :]
    blended = (resample(tiles[0], fraction_row) * weight).astype(jnp.bfloat16)
    owners = jnp.arange(group_size, dtype=jnp.int32)
    planes = jnp.arange(per_slab, dtype=jnp.int32)
    own_z = slab_index * GROUPZ + owners[:, None] * per_slab + planes[None, :]
    every = jnp.ones(own_z.shape, bool)
    own_planes = take_planes(blended, own_z - corner[0], every)
    tile_ranks = jnp.arange(group_size, dtype=jnp.int32)
    margin = MARGIN + JIT
    rim_above = shifted_2(blended[:margin], "slab", -1)
    rim_below = shifted_2(blended[depth - margin :], "slab", 1)
    neighbour_rows = lookup_rows(
        offsets,
        jnp.clip(jnp.stack([self_id - group_size, self_id + group_size]), 0, tile_total - 1),
    )
    below_pos = own_z - (neighbour_rows[0, 0] + depth - margin)
    above_pos = own_z - neighbour_rows[1, 0]
    lower_half = (owners < group_size // 2)[:, None]
    rim_planes = jnp.concatenate([rim_below, rim_above], axis=0)
    rim_pos = jnp.where(lower_half, below_pos, margin + above_pos)
    rim_usable = jnp.where(
        lower_half, (below_pos >= 0) & (below_pos < margin), (above_pos >= 0) & (above_pos < margin)
    )
    extra_planes = take_planes(rim_planes, rim_pos, rim_usable)
    outgoing = jnp.stack([own_planes, extra_planes], axis=1)
    received = lax.all_to_all(outgoing, "tile", split_axis=0, concat_axis=0, tiled=True)
    pieces = jnp.concatenate([received[:, 0], received[:, 1]], axis=0)
    side_group = jnp.where(owner_index < group_size // 2, slab_index - 1, slab_index + 1)
    source_group = jnp.concatenate(
        [
            jnp.full((group_size,), slab_index, jnp.int32),
            jnp.full((group_size,), side_group, jnp.int32),
        ]
    )
    source_rank = jnp.concatenate([tile_ranks, tile_ranks])
    group_valid = (source_group >= 0) & (source_group < group_total)
    source_id = jnp.clip(source_group * group_size + source_rank, 0, tile_total - 1)
    source_rows = lookup_rows(offsets, source_id)
    slab_z = self_id * per_slab + planes
    plane_pos = slab_z[None, :] - source_rows[:, 0:1]
    plane_inside = group_valid[:, None] & (plane_pos >= 0) & (plane_pos < depth)
    weight_z = jnp.where(
        plane_inside, ramp_at(jnp.clip(plane_pos, 0, depth - 1), depth, 2 * MARGIN), 0.0
    )
    volume_rows = (group_size - 1) * STEPY + tile_rows
    row_grid = jnp.arange(volume_rows, dtype=jnp.int32)
    row_pos = row_grid[None, :] - source_rows[:, 1:2]
    row_inside = (row_pos >= 0) & (row_pos < tile_rows)
    weight_y = jnp.where(
        row_inside, ramp_at(jnp.clip(row_pos, 0, tile_rows - 1), tile_rows, RY), 0.0
    )
    piece_count = pieces.shape[0]
    target_rows = jnp.clip(
        source_rows[:, 1:2] + jnp.arange(tile_rows, dtype=jnp.int32)[None, :], 0, volume_rows - 1
    )
    flat_rows = (
        jnp.transpose(pieces, (0, 2, 1, 3))
        .reshape(piece_count * tile_rows, per_slab * columns)
        .astype(jnp.float32)
    )
    placed = jax.ops.segment_sum(flat_rows, target_rows.reshape(-1), num_segments=volume_rows)
    numer = jnp.transpose(placed.reshape(volume_rows, per_slab, columns), (1, 0, 2))
    weight_plane = jnp.einsum("kz,ka->za", weight_z, weight_y, precision=lax.Precision.HIGHEST)
    weight_sum = weight_plane[:, :, None] * ramp_x[None, None, :]
    return (numer / jnp.maximum(weight_sum, weight_floor)).astype(jnp.bfloat16)


def solution(mesh):
    in_specs = (P(("slab", "tile"), None, None, None), P(), P())
    out_specs = P(("slab", "tile"), None, None)
    return jax.shard_map(shards, mesh=mesh, in_specs=in_specs, out_specs=out_specs, check_vma=False)
```

profile of v0, /device:TPU:1, one launch (start us, length us, event | category | flops | bytes accessed | tf_op | source)
XLA Modules:
  0.0 142.8 jit_solution(10713076276606054559)
XLA Ops:
  0.0 0.0 copy-start
  0.0 0.1 fusion.57
  0.1 0.1 fusion.43
  0.1 0.1 fusion.62
  0.2 0.5 copy-done
  0.7 0.1 constant_dynamic-slice_fusion
  0.8 0.6 fusion.126
  2.0 1.6 %convert_element_type.88 = f32[1,20,256,128]{3,2,1,0:T(8,128)S(1)} convert(bf16[1,20,256,128]{3,2,1,0:T(8,128)(2,1)} %param.3) | non-fusion elementwise | flops 655360 | bytes 3932160 | tf_op jit(solution)/shard_map/convert_element_type | solution.py:40
  3.6 0.2 slice_bitcast_fusion
  3.8 1.8 %bitcast_add_fusion = f32[20,256,128]{2,1,0:T(8,128)S(1)} fusion(f32[19,256,128]{2,1,0:T(8,128)S(1)} %slice_bitcast_fusion, f32[]{:T(128)} %bitcast.4, f32[]{:T(128)S(6)} %sub.226, bf16[1,20,256,128]{3,2,1,0:T(8,128)(2,1)} %param.3), kind=kLoop, calls=%fused_computation.5 | loop fusion | flops 2621440 | bytes 6422536 | tf_op jit(solution)/shard_map/add | solution.py:51
  5.6 0.0 copy-start.1
  5.7 2.0 %slice.74 = f32[20,255,128]{2,1,0:T(8,128)} slice(f32[20,256,128]{2,1,0:T(8,128)S(1)} %bitcast_add_fusion), slice={[0:20], [1:256], [0:128]} | slice | bytes 5222400 | tf_op jit(solution)/shard_map/slice | solution.py:46
  7.6 0.3 copy-done.1
  8.7 2.9 %multiply_add_fusion = f32[20,256,128]{2,1,0:T(8,128)S(1)} fusion(f32[20,255,128]{2,1,0:T(8,128)} %slice.74, f32[20,256,128]{2,1,0:T(8,128)} %copy-done.1, f32[]{:T(128)} %bitcast.3, f32[]{:T(128)S(6)} %sub.225), kind=kLoop, calls=%fused_computation.7 | loop fusion | flops 1966080 | bytes 7854088 | tf_op jit(solution)/shard_map/add | solution.py:51
  11.6 2.3 %slice.75 = f32[20,256,127]{2,1,0:T(8,128)} slice(f32[20,256,128]{2,1,0:T(8,128)S(1)} %multiply_add_fusion), slice={[0:20], [0:256], [1:128]} | slice | bytes 5201920 | tf_op jit(solution)/shard_map/slice | solution.py:46
  14.5 0.1 broadcast_multiply_fusion
  14.5 0.0 copy-start.3
  14.6 2.4 %multiply_convert_fusion = bf16[20,256,128]{2,1,0:T(8,128)(2,1)S(1)} fusion(f32[20,256,127]{2,1,0:T(8,128)} %slice.75, f32[20,256,128]{2,1,0:T(8,128)S(1)} %multiply_add_fusion, f32[128]{0:T(128)S(1)} %fusion.57, f32[20,256]{1,0:T(8,128)S(1)} %broadcast_multiply_fusion, f32[]{:T(128)} %bitcast.2, f32[]{:T(128)S(6)} %sub.224), kind=kLoop, calls=%fused_computation.6 | loop fusion | flops 3932160 | bytes 6554120 | tf_op jit(solution)/shard_map/convert_element_type | solution.py:86
  16.9 0.0 copy-start.2
  16.9 1.1 copy-done.2
  18.0 4.0 %collective-permute-start = (bf16[3,256,128]{2,1,0:T(8,128)(2,1)S(1)}, bf16[3,256,128]{2,1,0:T(8,128)(2,1)S(1)}, u32[]{:S(2)}, u32[]{:S(2)}) collective-permute-start(bf16[3,256,128]{2,1,0:T(8,128)(2,1)S(1)} %get-tuple-element.7), channel_id=1, source_target_pairs={{0,16},{16,32},{32,48},{48,64},{64,80},{80,96},{96,112},{112,128},... | collective-permute-start | bytes 589832 | tf_op jit(solution)/shard_map/ppermute | solution.py:21
  22.0 1.3 collective-permute-start.1
  23.3 0.1 add_clamp_fusion
  23.4 0.1 iota_compare_fusion.1
  23.4 0.0 copy-done.3
  23.4 0.1 select_reduce_fusion.1
  23.6 0.6 fusion.127
  24.8 0.7 fusion.80
  25.5 0.7 compare_and_fusion
  26.2 0.1 constant_dynamic-slice_fusion.1
  26.3 0.5 slice.54
  26.8 0.7 fusion.79
  27.5 0.7 compare_and_fusion.1
  28.2 2.1 %gather_fusion = bf16[16,256,128]{2,1,0:T(8,128)(2,1)S(1)} fusion(bf16[20,256,128]{2,1,0:T(8,128)(2,1)} %copy-done.2, s32[1024]{0:T(1024)S(1)} %pad_clamp_fusion.1), kind=kCustom, calls=%fused_computation | custom fusion | bytes 2097216 | tf_op jit(solution)/shard_map/jit(_take)/gather | solution.py:65
  30.2 0.2 bitcast_select_fusion.1
  30.4 0.0 collective-permute-done
  30.4 0.0 collective-permute-done.1
  30.5 0.7 gather_fusion.1
  31.2 0.2 fusion.2
  31.5 1.5 %pad_maximum_fusion = bf16[16,2,1,256,128]{4,3,2,1,0:T(8,128)(2,1)} fusion(bf16[16,1,1,256,128]{4,3,2,1,0:T(8,128)(2,1)S(1)} %fusion.2, bf16[16,1,1,256,128]{4,3,2,1,0:T(8,128)(2,1)S(1)} %bitcast_select_fusion.1), kind=kLoop, calls=%fused_computation.9 | loop fusion | flops 1048576 | bytes 4194304 | tf_op jit(solution)/shard_map/stack | solution.py:109
  33.0 11.4 %all-to-all-start = ((bf16[16,2,1,256,128]{4,3,2,1,0:T(8,128)(2,1)}), bf16[16,2,1,256,128]{4,3,2,1,0:T(8,128)(2,1)S(1)}, u32[]{:S(2)}, u32[]{:S(2)}) async-start(bf16[16,2,1,256,128]{4,3,2,1,0:T(8,128)(2,1)} %pad_maximum_fusion), calls=%async_computation | async-start | bytes 4194304 | tf_op jit(solution)/shard_map/all_to_all | solution.py:110
  44.4 0.1 fusion.81
  44.5 0.1 iota_compare_fusion
  44.5 0.1 select_reduce_fusion
  44.7 0.1 clamp_bitcast_fusion
  44.8 3.9 %convolution_reduce_fusion = f32[3706]{0:T(1024)S(1)} fusion(s32[32]{0:T(128)S(1)} %slice_bitcast_fusion.3, s32[32,2]{0,1:T(2,128)S(1)} %select_reduce_fusion, s32[16]{0:T(128)S(1)} %broadcast_in_dim.117, s32[]{:T(128)S(6)} %select_n.207, s32[]{:T(128)S(6)} %add.242), kind=kOutput, calls=%fused_computation.12 | convolution fusion | flops 4032960 | bytes 16368 | tf_op jit(solution)/shard_map/kz,ka->za/dot_general | solution.py:147
  48.7 44.7 %all-to-all-done = bf16[16,2,1,256,128]{4,3,2,1,0:T(8,128)(2,1)S(1)} async-done(((bf16[16,2,1,256,128]{4,3,2,1,0:T(8,128)(2,1)}), bf16[16,2,1,256,128]{4,3,2,1,0:T(8,128)(2,1)S(1)}, u32[]{:S(2)}, u32[]{:S(2)}) %all-to-all-start) | async-done | bytes 2097184 | tf_op jit(solution)/shard_map/all_to_all | solution.py:110
  93.3 0.1 slice_bitcast_fusion.2
  93.5 0.2 pad_maximum_fusion.1
  93.7 45.5 %scatter_custom_fusion = f32[3706,128]{1,0:T(8,128)} fusion(s32[8192]{0:T(1024)S(1)} %bitcast.46, bf16[8192,128]{1,0:T(8,128)(2,1)S(1)} %bitcast.45, f32[]{:T(128)} %constant.51.clone.1), kind=kCustom, calls=%fused_computation.3 | custom fusion | flops 2097152 | bytes 3994628 | tf_op jit(solution)/shard_map/scatter-add | solution.py:145
  139.2 3.6 %fusion.4 = bf16[1,3706,128]{2,1,0:T(8,128)(2,1)} fusion(f32[3706,128]{1,0:T(8,128)} %scatter_custom_fusion, f32[128]{0:T(128)S(1)} %fusion.57, f32[3706]{0:T(1024)S(1)} %convolution_reduce_fusion), kind=kLoop, calls=%fused_computation.19 | loop fusion | flops 1897472 | bytes 2861544 | tf_op jit(solution)/shard_map/convert_element_type | solution.py:149
  (8 shorter events, 0.1 us)
Async XLA Ops:
  0.0 0.7 copy-start
  5.6 2.3 %copy-start.1 = (f32[20,256,128]{2,1,0:T(8,128)}, f32[20,256,128]{2,1,0:T(8,128)S(1)}, u32[]{:S(2)}) copy-start(f32[20,256,128]{2,1,0:T(8,128)S(1)} %bitcast_add_fusion) | copy-start | bytes 7864324
  14.5 8.9 %copy-start.3 = (s32[768,2]{0,1:T(2,128)S(1)}, s32[768,2]{0,1:T(2,128)}, u32[]{:S(2)}) copy-start(s32[768,2]{0,1:T(2,128)} %param.4) | copy-start | bytes 18436
  16.9 1.1 copy-start.2
  18.0 12.4 %collective-permute-start = (bf16[3,256,128]{2,1,0:T(8,128)(2,1)S(1)}, bf16[3,256,128]{2,1,0:T(8,128)(2,1)S(1)}, u32[]{:S(2)}, u32[]{:S(2)}) collective-permute-start(bf16[3,256,128]{2,1,0:T(8,128)(2,1)S(1)} %get-tuple-element.7), channel_id=1, source_target_pairs={{0,16},{16,32},{32,48},{48,64},{64,80},{80,96},{96,112},{112,128},... | collective-permute-start | bytes 589832 | tf_op jit(solution)/shard_map/ppermute | solution.py:21
  22.0 8.4 %collective-permute-start.1 = (bf16[3,256,128]{2,1,0:T(8,128)(2,1)S(1)}, bf16[3,256,128]{2,1,0:T(8,128)(2,1)S(1)}, u32[]{:S(2)}, u32[]{:S(2)}) collective-permute-start(bf16[3,256,128]{2,1,0:T(8,128)(2,1)S(1)} %get-tuple-element.8), channel_id=1, source_target_pairs={{16,0},{32,16},{48,32},{64,48},{80,64},{96,80},{112,96},{128,112},... | collective-permute-start | bytes 589832 | tf_op jit(solution)/shard_map/ppermute | solution.py:21
  33.0 60.3 %all-to-all-start = ((bf16[16,2,1,256,128]{4,3,2,1,0:T(8,128)(2,1)}), bf16[16,2,1,256,128]{4,3,2,1,0:T(8,128)(2,1)S(1)}, u32[]{:S(2)}, u32[]{:S(2)}) async-start(bf16[16,2,1,256,128]{4,3,2,1,0:T(8,128)(2,1)} %pad_maximum_fusion), calls=%async_computation | async-start | bytes 4194304 | tf_op jit(solution)/shard_map/all_to_all | solution.py:110
where the time goes:
time: 144 us; the launch traced here: 143 us
  other arithmetic  63.5 us (44%)
  waiting for transfers between devices  44.7 us (31%)
  starting transfers between devices  16.6 us (12%)
  local copies, waits for them, and re-layouts  11.2 us (8%)
  matrix products  3.89 us (3%)
  between operations  2.9 us (2%)
    scatter-add x1, other arithmetic, shards(): jax.ops.segment_sum(flat_rows, target_rows.reshape(-1), num_segments=volu...  45.5 us
    all_to_all x1, waiting for transfers between devices, shards(): lax.all_to_all(outgoing, 'tile', split_axis=0, concat_axis=0, tiled=True)  44.7 us
    all_to_all x1, starting transfers between devices, shards(): lax.all_to_all(outgoing, 'tile', split_axis=0, concat_axis=0, tiled=True)  11.4 us
    ppermute x2, starting transfers between devices, shifted_2(): return lax.ppermute(block, axis, route)  5.25 us
    add x2, other arithmetic, resample(): volume_field = (1.0 - fraction) * volume_field + fraction * shifted  4.71 us
    slice x3, local copies, waits for them, and re-layouts, resample(): lax.slice_in_dim(volume_field, 1, extent, axis=direction)  4.41 us
    dot_general x1, matrix products, shards(): jnp.einsum('kz,ka->za', weight_z, weight_y, precision=lax.Precision.HIGHEST)  3.89 us
    convert_element_type x1, other arithmetic, shards(): return (numer / jnp.maximum(weight_sum, weight_floor)).astype(jnp.bfloat16)  3.59 us
  transfers between devices with their start and end apart: 3, of which 1 were waited for; matrix products, arithmetic and copies ran while one was open for 7% of the time, Pallas kernels for 0%

commit v1 on v0

v1 whole, which is shorter than its diff:
```python
import functools

import jax
import jax.numpy as jnp
import numpy as np
from jax import lax
from jax.experimental import pallas as pl
from jax.experimental.pallas import tpu as pltpu
from jax.sharding import PartitionSpec as P

GROUPZ = 16
MARGIN = 2
JIT = 1
RIM = MARGIN + JIT
TY = 256
TX = 128
TZ = 20
STEPY = 230
JITY = 4
RY = 26
RX = 16
QUANT = 16
RANKS = 16
MY = 3706
FLOOR = 0.05

FRAME = 272
PAD = 16
SPAN = 16 + FRAME + 16
MYP = 3712

BASES = [max(0, (STEPY * r - JITY) // 8 * 8) for r in range(RANKS)]
LOW = tuple(range(RIM))
HIGH = tuple(range(GROUPZ - RIM, GROUPZ))

VMEM = pl.BlockSpec(memory_space=pltpu.VMEM)
SMEM = pl.BlockSpec(memory_space=pltpu.SMEM)
ANY = pl.BlockSpec(memory_space=pl.ANY)


def ramp(length, ramp_width):
    position = np.arange(length, dtype=np.float64)
    rising = 0.5 - 0.5 * np.cos(np.pi * (position + 1.0) / (ramp_width + 1.0))
    rising = np.where(position < ramp_width, rising, 1.0)
    return np.minimum(rising, rising[::-1]).astype(np.float32)


RAMP_Z = [float(v) for v in ramp(TZ, 2 * MARGIN)]


def row_table():
    table = np.zeros((SPAN, TX), np.float32)
    table[PAD : PAD + TY] = ramp(TY, RY)[:, None]
    return jnp.asarray(table)


def column_table():
    wx = ramp(TX, RX)
    cut = wx.copy()
    cut[-1] = 0.0
    table = np.zeros((8, TX), np.float32)
    table[0], table[1] = wx, cut
    return jnp.asarray(table)


def weight_z(plane):
    near = jnp.minimum(plane, TZ - 1 - plane)
    value = jnp.where(near < 0, jnp.float32(0.0), jnp.float32(1.0))
    for i in range(2 * MARGIN):
        value = jnp.where(near == i, jnp.float32(RAMP_Z[i]), value)
    return value


def base_of(rank):
    return jnp.maximum((STEPY * rank - JITY) // 8 * 8, 0)


def spot():
    return lax.axis_index("slab"), lax.axis_index("tile")


def fraction(fracs_ref, tile, direction):
    return fracs_ref[direction, tile].astype(jnp.float32) * (1.0 / QUANT)


def rims_kernel(tiles_ref, fracs_ref, low_ref, high_ref, held, sems):
    slab, rank = spot()
    tile = slab * RANKS + rank
    first = pltpu.make_async_copy(tiles_ref.at[0, pl.ds(0, RIM + 1)], held.at[pl.ds(0, RIM + 1)], sems.at[0])
    last = pltpu.make_async_copy(tiles_ref.at[0, pl.ds(TZ - RIM, RIM)], held.at[pl.ds(RIM + 1, RIM)], sems.at[1])
    first.start()
    last.start()
    f = fraction(fracs_ref, tile, 0)
    first.wait()
    for p in range(RIM):
        low_ref[p] = ((1.0 - f) * held[p].astype(jnp.float32) + f * held[p + 1].astype(jnp.float32)).astype(jnp.bfloat16)
    last.wait()
    for p in range(RIM):
        here = (1.0 - f) * held[RIM + 1 + p].astype(jnp.float32)
        if p < RIM - 1:
            here = here + f * held[RIM + 2 + p].astype(jnp.float32)
        high_ref[p] = here.astype(jnp.bfloat16)


def row_terms(table_ref, terms, shift, f):
    w = table_ref[pl.ds(PAD - shift, FRAME), :]
    terms[0] = (1.0 - f) * w
    terms[1] = f * w


def blend(held, slot, terms, shift, c0, c1):
    u = held[slot, pl.ds(PAD - shift, FRAME), :] * terms[0] + held[slot, pl.ds(PAD + 1 - shift, FRAME), :] * terms[1]
    return u * c0 + pltpu.roll(u, TX - 1, 1) * c1


def own_kernel(tiles_ref, offsets_ref, fracs_ref, table_ref, cols_ref, out_ref, rim_ref, held, terms, sent, sems):
    slab, rank = spot()
    tile = slab * RANKS + rank
    shift = offsets_ref[1, tile] - base_of(rank)
    first = slab * GROUPZ - offsets_ref[0, tile]
    fz, fy, fx = [fraction(fracs_ref, tile, d) for d in range(3)]
    row_terms(table_ref, terms, shift, fy)
    c0 = (1.0 - fx) * cols_ref[0:1, :]
    c1 = fx * cols_ref[1:2, :]
    for slot in range(2):
        held[slot, 0:PAD, :] = jnp.zeros((PAD, TX), jnp.float32)
        held[slot, PAD + TY : SPAN, :] = jnp.zeros((SPAN - PAD - TY, TX), jnp.float32)

    def plane(z, slot):
        p = first + z
        w = weight_z(p)
        held[slot, PAD : PAD + TY, :] = (w * (1.0 - fz)) * tiles_ref[0, p].astype(jnp.float32) + (w * fz) * tiles_ref[
            0, p + 1
        ].astype(jnp.float32)
        return blend(held, slot, terms, shift, c0, c1)

    for i, z in enumerate(LOW + HIGH):
        rim_ref[i] = plane(z, i % 2)
    copies = []
    for i in range(GROUPZ - 2 * RIM):
        sent[i] = plane(RIM + i, i % 2).astype(jnp.bfloat16)
        copies.append(pltpu.make_async_copy(sent.at[i], out_ref.at[RIM + i], sems.at[i]))
        copies[-1].start()
    for copy in copies:
        copy.wait()


def merge_kernel(frames_ref, rim_ref, below_ref, above_ref, offsets_ref, fracs_ref, table_ref, cols_ref, out_ref, held, terms, sent, sems):
    slab, rank = spot()
    last = lax.axis_size("slab") - 1
    for slot in range(2):
        held[slot, 0:PAD, :] = jnp.zeros((PAD, TX), jnp.float32)
        held[slot, PAD + TY : SPAN, :] = jnp.zeros((SPAN - PAD - TY, TX), jnp.float32)
    for side, (planes, source_ref) in enumerate(((LOW, below_ref), (HIGH, above_ref))):
        group = slab - 1 if side == 0 else slab + 1
        valid = jnp.logical_and(group >= 0, group <= last)
        tile = jnp.clip(group, 0, last) * RANKS + rank
        shift = offsets_ref[1, tile] - base_of(rank)
        first = slab * GROUPZ - offsets_ref[0, tile]
        first = jnp.where(valid, first, 2 * TZ)
        row_terms(table_ref, terms, shift, fraction(fracs_ref, tile, 1))
        fx = fraction(fracs_ref, tile, 2)
        c0 = (1.0 - fx) * cols_ref[0:1, :]
        c1 = fx * cols_ref[1:2, :]
        for i, z in enumerate(planes):
            p = first + z
            w = weight_z(p)
            at = jnp.clip(p - (TZ - RIM) if side == 0 else p, 0, RIM - 1)
            held[i % 2, PAD : PAD + TY, :] = w * source_ref[at].astype(jnp.float32)
            total = rim_ref[side * RIM + i] + blend(held, i % 2, terms, shift, c0, c1)
            sent[side * RIM + i] = total.astype(jnp.bfloat16)
    copies = []
    for side, planes in enumerate((LOW, HIGH)):
        copies.append(
            pltpu.make_async_copy(sent.at[pl.ds(side * RIM, RIM)], out_ref.at[pl.ds(planes[0], RIM)], sems.at[side])
        )
        copies[-1].start()
    for copy in copies:
        copy.wait()


def weights_kernel(offsets_ref, table_ref, cols_ref, out_ref):
    slab, rank = spot()
    last = lax.axis_size("slab") - 1
    z = slab * GROUPZ + rank
    side = jnp.where(rank < RANKS // 2, slab - 1, slab + 1)
    valid = jnp.logical_and(side >= 0, side <= last)
    out_ref[...] = jnp.zeros_like(out_ref)
    for r in range(RANKS):
        total = 0.0
        for group, usable in ((slab, None), (jnp.clip(side, 0, last), valid)):
            tile = group * RANKS + r
            w = weight_z(z - offsets_ref[0, tile])
            if usable is not None:
                w = jnp.where(usable, w, 0.0)
            total = total + w * table_ref[pl.ds(PAD + BASES[r] - offsets_ref[1, tile], FRAME), :]
        out_ref[BASES[r] : BASES[r] + FRAME, :] += total
    out_ref[...] = 1.0 / jnp.maximum(out_ref[...] * cols_ref[0:1, :], FLOOR)


def join_kernel(frames_ref, recip_ref, out_ref, held):
    done = 0
    for r in range(RANKS):
        base = BASES[r]
        for k in range(0, FRAME, 16):
            piece = frames_ref[r, k : k + 16, :].astype(jnp.float32)
            for h in (0, 8):
                row = base + k + h
                part = piece[h : h + 8]
                if row < done:
                    held[row : row + 8, :] += part
                else:
                    held[row : row + 8, :] = part
        done = base + FRAME
    for k in range(0, MY, 16):
        n = min(16, MY - k)
        out_ref[0, k : k + n, :] = (held[k : k + n, :] * recip_ref[k : k + n, :]).astype(jnp.bfloat16)


def cost(flops, moved):
    return pl.CostEstimate(flops=flops, bytes_accessed=moved, transcendentals=0)


def beside(block, distance):
    devices = range(lax.axis_size("slab"))
    return lax.ppermute(block, "slab", [(i, i + distance) for i in devices if i + distance in devices])


def shards(tiles, offsets, fracs):
    call = functools.partial(pl.pallas_call)
    params = pltpu.CompilerParams(vmem_limit_bytes=32 * 2**20)
    shape = jax.ShapeDtypeStruct
    offsets, fracs = offsets.T, fracs.T
    rows, cols = row_table(), column_table()
    rim = shape((RIM, TY, TX), jnp.bfloat16)
    work = [pltpu.VMEM((2, SPAN, TX), jnp.float32), pltpu.VMEM((2, FRAME, TX), jnp.float32)]
    frames = shape((RANKS, FRAME, TX), jnp.bfloat16)

    low, high = call(
        rims_kernel,
        out_shape=(rim, rim),
        in_specs=[ANY, SMEM],
        out_specs=(VMEM, VMEM),
        scratch_shapes=[pltpu.VMEM((2 * RIM + 1, TY, TX), jnp.bfloat16), pltpu.SemaphoreType.DMA((2,))],
        compiler_params=params,
        cost_estimate=cost(10**6, 10**6),
        name="rims",
    )(tiles, fracs)
    above = beside(low, -1)
    below = beside(high, 1)
    own, own_rim = call(
        own_kernel,
        out_shape=(frames, shape((2 * RIM, FRAME, TX), jnp.float32)),
        in_specs=[VMEM, SMEM, SMEM, VMEM, VMEM],
        out_specs=(ANY, VMEM),
        scratch_shapes=[*work, pltpu.VMEM((GROUPZ - 2 * RIM, FRAME, TX), jnp.bfloat16), pltpu.SemaphoreType.DMA((GROUPZ - 2 * RIM,))],
        compiler_params=params,
        cost_estimate=cost(10**7, 3 * 10**6),
        name="own",
    )(tiles, offsets, fracs, rows, cols)
    merged = call(
        merge_kernel,
        out_shape=frames,
        in_specs=[ANY, VMEM, VMEM, VMEM, SMEM, SMEM, VMEM, VMEM],
        out_specs=ANY,
        scratch_shapes=[*work, pltpu.VMEM((2 * RIM, FRAME, TX), jnp.bfloat16), pltpu.SemaphoreType.DMA((2,))],
        input_output_aliases={0: 0},
        compiler_params=params,
        cost_estimate=cost(3 * 10**6, 2 * 10**6),
        name="merge",
    )(own, own_rim, below, above, offsets, fracs, rows, cols)
    received = lax.all_to_all(merged, "tile", split_axis=0, concat_axis=0, tiled=True)
    recip = call(
        weights_kernel,
        out_shape=shape((MYP, TX), jnp.float32),
        in_specs=[SMEM, VMEM, VMEM],
        out_specs=VMEM,
        compiler_params=params,
        cost_estimate=cost(10**7, 4 * 10**6),
        name="weights",
    )(offsets, rows, cols)
    return call(
        join_kernel,
        out_shape=shape((1, MY, TX), jnp.bfloat16),
        in_specs=[VMEM, VMEM],
        out_specs=VMEM,
        scratch_shapes=[pltpu.VMEM((MYP, TX), jnp.float32)],
        compiler_params=params,
        cost_estimate=cost(10**6, 4 * 10**6),
        name="join",
    )(received, recip)


def solution(mesh):
    in_specs = (P(("slab", "tile"), None, None, None), P(), P())
    out_specs = P(("slab", "tile"), None, None)
    return jax.shard_map(shards, mesh=mesh, in_specs=in_specs, out_specs=out_specs, check_vma=False)
```

time: 144 us -> 60.9 us (0.42)
  the two profiles are of different devices: /device:TPU:1 before, /device:TPU:199 now
where the time goes in v1:
time: 60.9 us; the launch traced here: 60.6 us
  waiting for transfers between devices  33.8 us (56%)
  starting transfers between devices  16 us (26%)
  Pallas kernels  8.61 us (14%)
  local copies, waits for them, and re-layouts  2.04 us (3%)
    all_to_all x1, waiting for transfers between devices, shards(): lax.all_to_all(merged, 'tile', split_axis=0, concat_axis=0, tiled=True)  28 us
    all_to_all x1, starting transfers between devices, shards(): lax.all_to_all(merged, 'tile', split_axis=0, concat_axis=0, tiled=True)  8.98 us
    ppermute x2, starting transfers between devices, beside(): lax.ppermute(block, 'slab', [(i, i + distance) for i in devices if i + di...  7.05 us
    ppermute x2, waiting for transfers between devices, beside(): lax.ppermute(block, 'slab', [(i, i + distance) for i in devices if i + di...  5.82 us
    pallas_call x1, Pallas kernels, shards(): call(own_kernel, out_shape=(frames, shape((2 * RIM, FRAME, TX), jnp.float...  2.86 us
    pallas_call x1, Pallas kernels, shards(): call(merge_kernel, out_shape=frames, in_specs=[ANY, VMEM, VMEM, VMEM, SME...  2.15 us
    unnamed x12, local copies, waits for them, and re-layouts  2.04 us
    pallas_call x1, Pallas kernels, shards(): call(weights_kernel, out_shape=shape((MYP, TX), jnp.float32), in_specs=[S...  1.23 us
  transfers between devices with their start and end apart: 3, of which 2 were waited for; matrix products, arithmetic and copies ran while one was open for 0% of the time, Pallas kernels for 7%

profile of v1, /device:TPU:199, one launch (start us, length us, event | category | flops | bytes accessed | tf_op | source)
XLA Modules:
  0.0 60.6 jit_solution(10986280431038522183)
XLA Ops:
  0.0 0.0 copy-start
  0.0 1.3 %copy-done = bf16[1,20,256,128]{3,2,1,0:T(8,128)(2,1)S(1)} copy-done((bf16[1,20,256,128]{3,2,1,0:T(8,128)(2,1)S(1)}, bf16[1,20,256,128]{3,2,1,0:T(8,128)(2,1)}, u32[]{:S(2)}) %copy-start) | copy-done | bytes 1310744
  1.3 0.0 copy-start.2
  1.3 0.7 %copy-done.2 = s32[768,3]{0,1:T(4,128)S(1)} copy-done((s32[768,3]{0,1:T(4,128)S(1)}, s32[768,3]{0,1:T(4,128)}, u32[]{:S(2)}) %copy-start.2) | copy-done | bytes 9240
  2.0 0.0 copy-start.1
  2.0 0.0 copy-start.3
  2.0 0.0 copy-start.4
  2.0 0.0 copy-start.5
  2.0 1.2 %rims.1 = (bf16[3,256,128]{2,1,0:T(8,128)(2,1)S(1)}, bf16[3,256,128]{2,1,0:T(8,128)(2,1)S(1)}) custom-call(bf16[1,20,256,128]{3,2,1,0:T(8,128)(2,1)S(1)} %copy-done, s32[3,768]{1,0:T(4,128)S(1)} %bitcast.2), custom_call_target="tpu_custom_call" | custom-call | flops 1000000 | bytes 1000000 | tf_op jit(solution)/shard_map/rims/pallas_call | solution.py:239
  3.2 5.1 %collective-permute-start = (bf16[3,256,128]{2,1,0:T(8,128)(2,1)S(1)}, bf16[3,256,128]{2,1,0:T(8,128)(2,1)S(1)}, u32[]{:S(2)}, u32[]{:S(2)}) collective-permute-start(bf16[3,256,128]{2,1,0:T(8,128)(2,1)S(1)} %get-tuple-element.11), channel_id=1, source_target_pairs={{0,16},{16,32},{32,48},{48,64},{64,80},{80,96},{96,112},{112,128},... | collective-permute-start | bytes 589832 | tf_op jit(solution)/shard_map/ppermute | solution.py:226
  8.3 1.9 %collective-permute-start.1 = (bf16[3,256,128]{2,1,0:T(8,128)(2,1)S(1)}, bf16[3,256,128]{2,1,0:T(8,128)(2,1)S(1)}, u32[]{:S(2)}, u32[]{:S(2)}) collective-permute-start(bf16[3,256,128]{2,1,0:T(8,128)(2,1)S(1)} %get-tuple-element.12), channel_id=1, source_target_pairs={{16,0},{32,16},{48,32},{64,48},{80,64},{96,80},{112,96},{128,112},... | collective-permute-start | bytes 589832 | tf_op jit(solution)/shard_map/ppermute | solution.py:226
  10.3 0.0 copy-done.1
  10.3 0.0 copy-done.3
  10.3 0.0 copy-done.4
  10.3 0.0 copy-done.5
  10.3 2.9 %own.1 = (bf16[16,272,128]{2,1,0:T(8,128)(2,1)}, f32[6,272,128]{2,1,0:T(8,128)S(1)}) custom-call(bf16[1,20,256,128]{3,2,1,0:T(8,128)(2,1)S(1)} %copy-done, s32[2,768]{1,0:T(2,128)S(1)} %bitcast.5, s32[3,768]{1,0:T(4,128)S(1)} %bitcast.3, f32[304,128]{1,0:T(8,128)S(1)} %copy-done.1, f32[8,128]{1,0:T(8,128)S(1)} %copy-done.5), custom_call_target="tpu_custom_call" | custom-call | flops 10000000 | bytes 3000000 | tf_op jit(solution)/shard_map/own/pallas_call | solution.py:251
  13.2 0.0 collective-permute-done.below_ref
  13.2 5.8 %collective-permute-done.1.above_ref = bf16[3,256,128]{2,1,0:T(8,128)(2,1)S(1)} collective-permute-done((bf16[3,256,128]{2,1,0:T(8,128)(2,1)S(1)}, bf16[3,256,128]{2,1,0:T(8,128)(2,1)S(1)}, u32[]{:S(2)}, u32[]{:S(2)}) %collective-permute-start.1) | collective-permute-done | bytes 196640 | tf_op jit(solution)/shard_map/ppermute | solution.py:226
  19.0 2.2 %merge.1 = bf16[16,272,128]{2,1,0:T(8,128)(2,1)} custom-call(bf16[16,272,128]{2,1,0:T(8,128)(2,1)} %get-tuple-element.9.frames_ref, f32[6,272,128]{2,1,0:T(8,128)S(1)} %get-tuple-element.10.rim_ref, bf16[3,256,128]{2,1,0:T(8,128)(2,1)S(1)} %collective-permute-done.below_ref, ...), custom_call_target="tpu_custom_call", output_to_operand_aliasing={{}: (0, {})} | custom-call | flops 3000000 | bytes 2000000 | tf_op jit(solution)/shard_map/merge/pallas_call | solution.py:261
  21.2 9.0 %all-to-all-start = ((bf16[16,272,128]{2,1,0:T(8,128)(2,1)}), bf16[16,272,128]{2,1,0:T(8,128)(2,1)S(1)}, u32[]{:S(2)}, u32[]{:S(2)}) async-start(bf16[16,272,128]{2,1,0:T(8,128)(2,1)} %merge.1), calls=%async_computation | async-start | bytes 2228224 | tf_op jit(solution)/shard_map/all_to_all | solution.py:272
  30.2 1.2 %weights.1.recip_ref = f32[3712,128]{1,0:T(8,128)S(1)} custom-call(s32[2,768]{1,0:T(2,128)S(1)} %bitcast.7, f32[304,128]{1,0:T(8,128)S(1)} %copy-done.1, f32[8,128]{1,0:T(8,128)S(1)} %copy-done.5), custom_call_target="tpu_custom_call" | custom-call | flops 10000000 | bytes 4000000 | tf_op jit(solution)/shard_map/weights/pallas_call | solution.py:273
  31.4 28.0 %all-to-all-done.frames_ref = bf16[16,272,128]{2,1,0:T(8,128)(2,1)S(1)} async-done(((bf16[16,272,128]{2,1,0:T(8,128)(2,1)}), bf16[16,272,128]{2,1,0:T(8,128)(2,1)S(1)}, u32[]{:S(2)}, u32[]{:S(2)}) %all-to-all-start) | async-done | bytes 1114144 | tf_op jit(solution)/shard_map/all_to_all | solution.py:272
  59.4 1.2 %join.1 = bf16[1,3706,128]{2,1,0:T(8,128)(2,1)} custom-call(bf16[16,272,128]{2,1,0:T(8,128)(2,1)S(1)} %all-to-all-done.frames_ref, f32[3712,128]{1,0:T(8,128)S(1)} %weights.1.recip_ref), custom_call_target="tpu_custom_call" | custom-call | flops 1000000 | bytes 4000000 | tf_op jit(solution)/shard_map/join/pallas_call | solution.py:282
Async XLA Ops:
  0.0 1.3 %copy-start = (bf16[1,20,256,128]{3,2,1,0:T(8,128)(2,1)S(1)}, bf16[1,20,256,128]{3,2,1,0:T(8,128)(2,1)}, u32[]{:S(2)}) copy-start(bf16[1,20,256,128]{3,2,1,0:T(8,128)(2,1)} %tiles_ref.3) | copy-start | bytes 3932164
  1.3 0.7 %copy-start.2 = (s32[768,3]{0,1:T(4,128)S(1)}, s32[768,3]{0,1:T(4,128)}, u32[]{:S(2)}) copy-start(s32[768,3]{0,1:T(4,128)} %param.7) | copy-start | bytes 27652
  2.0 8.2 %copy-start.1 = (f32[304,128]{1,0:T(8,128)S(1)}, f32[304,128]{1,0:T(8,128)}, u32[]{:S(2)}) copy-start(f32[304,128]{1,0:T(8,128)} %constant.4.clone.table_ref) | copy-start | bytes 466948
  2.0 8.3 %copy-start.3 = (s32[768,3]{0,1:T(4,128)S(1)}, s32[768,3]{0,1:T(4,128)}, u32[]{:S(2)}) copy-start(s32[768,3]{0,1:T(4,128)} %param.7) | copy-start | bytes 27652
  2.0 8.3 %copy-start.4 = (s32[768,2]{0,1:T(2,128)S(1)}, s32[768,2]{0,1:T(2,128)}, u32[]{:S(2)}) copy-start(s32[768,2]{0,1:T(2,128)} %param.6) | copy-start | bytes 18436
  2.0 8.3 %copy-start.5 = (f32[8,128]{1,0:T(8,128)S(1)}, f32[8,128]{1,0:T(8,128)}, u32[]{:S(2)}) copy-start(f32[8,128]{1,0:T(8,128)} %constant.5.clone.cols_ref) | copy-start | bytes 12292
  3.2 10.0 %collective-permute-start = (bf16[3,256,128]{2,1,0:T(8,128)(2,1)S(1)}, bf16[3,256,128]{2,1,0:T(8,128)(2,1)S(1)}, u32[]{:S(2)}, u32[]{:S(2)}) collective-permute-start(bf16[3,256,128]{2,1,0:T(8,128)(2,1)S(1)} %get-tuple-element.11), channel_id=1, source_target_pairs={{0,16},{16,32},{32,48},{48,64},{64,80},{80,96},{96,112},{112,128},... | collective-permute-start | bytes 589832 | tf_op jit(solution)/shard_map/ppermute | solution.py:226
  8.3 10.7 %collective-permute-start.1 = (bf16[3,256,128]{2,1,0:T(8,128)(2,1)S(1)}, bf16[3,256,128]{2,1,0:T(8,128)(2,1)S(1)}, u32[]{:S(2)}, u32[]{:S(2)}) collective-permute-start(bf16[3,256,128]{2,1,0:T(8,128)(2,1)S(1)} %get-tuple-element.12), channel_id=1, source_target_pairs={{16,0},{32,16},{48,32},{64,48},{80,64},{96,80},{112,96},{128,112},... | collective-permute-start | bytes 589832 | tf_op jit(solution)/shard_map/ppermute | solution.py:226
  21.2 38.2 %all-to-all-start = ((bf16[16,272,128]{2,1,0:T(8,128)(2,1)}), bf16[16,272,128]{2,1,0:T(8,128)(2,1)S(1)}, u32[]{:S(2)}, u32[]{:S(2)}) async-start(bf16[16,272,128]{2,1,0:T(8,128)(2,1)} %merge.1), calls=%async_computation | async-start | bytes 2228224 | tf_op jit(solution)/shard_map/all_to_all | solution.py:272

commit v2 on v1

v2 whole, which is shorter than its diff:
```python
import functools

import jax
import jax.numpy as jnp
import numpy as np
from jax import lax
from jax.experimental import pallas as pl
from jax.experimental.pallas import tpu as pltpu
from jax.sharding import PartitionSpec as P

GROUPZ = 16
MARGIN = 2
JIT = 1
RIM = MARGIN + JIT
TY = 256
TX = 128
TZ = 20
STEPY = 230
JITY = 4
RY = 26
RX = 16
QUANT = 16
RANKS = 16
MY = 3706
FLOOR = 0.05

FRAME = TY + 2 * JITY
STRIP = 272
PAD = 16
SPAN = 16 + STRIP + 16
MYP = 3712

BASES = [max(0, STEPY * r - JITY) for r in range(RANKS)]
LOW = tuple(range(RIM))
HIGH = tuple(range(GROUPZ - RIM, GROUPZ))

VMEM = pl.BlockSpec(memory_space=pltpu.VMEM)
SMEM = pl.BlockSpec(memory_space=pltpu.SMEM)
ANY = pl.BlockSpec(memory_space=pl.ANY)
HBM = pl.BlockSpec(memory_space=pltpu.HBM)


def ramp(length, ramp_width):
    position = np.arange(length, dtype=np.float64)
    rising = 0.5 - 0.5 * np.cos(np.pi * (position + 1.0) / (ramp_width + 1.0))
    rising = np.where(position < ramp_width, rising, 1.0)
    return np.minimum(rising, rising[::-1]).astype(np.float32)


RAMP_Z = [float(v) for v in ramp(TZ, 2 * MARGIN)]


def row_table():
    table = np.zeros((SPAN, TX), np.float32)
    table[PAD : PAD + TY] = ramp(TY, RY)[:, None]
    return jnp.asarray(table)


def column_table():
    wx = ramp(TX, RX)
    cut = wx.copy()
    cut[-1] = 0.0
    table = np.zeros((8, TX), np.float32)
    table[0], table[1] = wx, cut
    return jnp.asarray(table)


def weight_z(plane):
    near = jnp.minimum(plane, TZ - 1 - plane)
    value = jnp.where(near < 0, jnp.float32(0.0), jnp.float32(1.0))
    for i in range(2 * MARGIN):
        value = jnp.where(near == i, jnp.float32(RAMP_Z[i]), value)
    return value


def base_of(rank):
    return jnp.maximum(STEPY * rank - JITY, 0)


def spot():
    return lax.axis_index("slab"), lax.axis_index("tile")


def fraction(fracs_ref, tile, direction):
    return fracs_ref[direction, tile].astype(jnp.float32) * (1.0 / QUANT)


def row_terms(table_ref, terms, shift, f):
    w = table_ref[pl.ds(PAD - shift, FRAME), :]
    terms[0] = (1.0 - f) * w
    terms[1] = f * w


def blend(held, slot, terms, shift, c0, c1):
    u = held[slot, pl.ds(PAD - shift, FRAME), :] * terms[0] + held[slot, pl.ds(PAD + 1 - shift, FRAME), :] * terms[1]
    return u * c0 + pltpu.roll(u, TX - 1, 1) * c1


def clear_edges(held):
    for slot in range(2):
        held[slot, 0:PAD, :] = jnp.zeros((PAD, TX), jnp.float32)
        held[slot, PAD + TY : SPAN, :] = jnp.zeros((SPAN - PAD - TY, TX), jnp.float32)


def tile_terms(offsets_ref, fracs_ref, table_ref, cols_ref, terms):
    slab, rank = spot()
    tile = slab * RANKS + rank
    shift = offsets_ref[1, tile] - base_of(rank)
    fz, fy, fx = [fraction(fracs_ref, tile, d) for d in range(3)]
    row_terms(table_ref, terms, shift, fy)
    return offsets_ref[0, tile], shift, fz, (1.0 - fx) * cols_ref[0:1, :], fx * cols_ref[1:2, :]


def rims_kernel(tiles_ref, offsets_hbm, fracs_hbm, table_hbm, cols_hbm, one_ref, two_ref, planes, offsets_ref, fracs_ref, table_ref, cols_ref, held, terms, sems):
    copies = [
        pltpu.make_async_copy(offsets_hbm, offsets_ref, sems.at[0]),
        pltpu.make_async_copy(fracs_hbm, fracs_ref, sems.at[1]),
        pltpu.make_async_copy(table_hbm, table_ref, sems.at[2]),
        pltpu.make_async_copy(cols_hbm, cols_ref, sems.at[3]),
        pltpu.make_async_copy(tiles_ref.at[0, pl.ds(0, RIM + 1)], planes.at[pl.ds(0, RIM + 1)], sems.at[4]),
        pltpu.make_async_copy(tiles_ref.at[0, pl.ds(TZ - RIM, RIM)], planes.at[pl.ds(RIM + 1, RIM)], sems.at[5]),
    ]
    for copy in copies:
        copy.start()
    clear_edges(held)
    for copy in copies:
        copy.wait()
    slab, _ = spot()
    origin, shift, fz, c0, c1 = tile_terms(offsets_ref, fracs_ref, table_ref, cols_ref, terms)
    for turn, out_ref in enumerate((one_ref, two_ref)):
        upward = slab % 2 != turn
        first = jnp.where(upward, (slab + 1) * GROUPZ, slab * GROUPZ - RIM) - origin
        skipped = jnp.where(upward, TZ - RIM - (RIM + 1), 0)
        for i in range(RIM):
            p = first + i
            w = weight_z(p)
            after = jnp.where(p < TZ - 1, w * fz, 0.0)
            here = jnp.clip(p - skipped, 0, 2 * RIM)
            there = jnp.clip(p + 1 - skipped, 0, 2 * RIM)
            held[i % 2, PAD : PAD + TY, :] = (w * (1.0 - fz)) * planes[here].astype(jnp.float32) + after * planes[
                there
            ].astype(jnp.float32)
            out_ref[i] = blend(held, i % 2, terms, shift, c0, c1).astype(jnp.bfloat16)


def own_kernel(tiles_ref, offsets_ref, fracs_ref, table_ref, cols_ref, out_ref, rim_ref, held, terms, sent, sems):
    slab, _ = spot()
    origin, shift, fz, c0, c1 = tile_terms(offsets_ref, fracs_ref, table_ref, cols_ref, terms)
    first = slab * GROUPZ - origin
    clear_edges(held)

    def plane(z, slot):
        p = first + z
        w = weight_z(p)
        held[slot, PAD : PAD + TY, :] = (w * (1.0 - fz)) * tiles_ref[0, p].astype(jnp.float32) + (w * fz) * tiles_ref[
            0, p + 1
        ].astype(jnp.float32)
        return blend(held, slot, terms, shift, c0, c1)

    copies = []
    for i in range(GROUPZ - 2 * RIM):
        sent[i] = plane(RIM + i, i % 2).astype(jnp.bfloat16)
        copies.append(pltpu.make_async_copy(sent.at[i], out_ref.at[RIM + i], sems.at[i]))
        copies[-1].start()
    for i, z in enumerate(LOW + HIGH):
        rim_ref[i] = plane(z, i % 2)
    for copy in copies:
        copy.wait()


def merge_kernel(frames_ref, rim_ref, one_ref, two_ref, out_ref, sent, sems):
    slab, _ = spot()
    copies = []
    for turn, source_ref in enumerate((one_ref, two_ref)):
        side = jnp.where(slab % 2 != turn, 1, 0)
        for i in range(RIM):
            sent[turn * RIM + i] = (rim_ref[side * RIM + i] + source_ref[i].astype(jnp.float32)).astype(jnp.bfloat16)
        copies.append(
            pltpu.make_async_copy(
                sent.at[pl.ds(turn * RIM, RIM)], out_ref.at[pl.ds(side * (GROUPZ - RIM), RIM)], sems.at[turn]
            )
        )
        copies[-1].start()
    for copy in copies:
        copy.wait()


def weights_kernel(offsets_ref, table_ref, cols_ref, out_ref):
    slab, rank = spot()
    last = lax.axis_size("slab") - 1
    z = slab * GROUPZ + rank
    side = jnp.where(rank < RANKS // 2, slab - 1, slab + 1)
    valid = jnp.logical_and(side >= 0, side <= last)
    out_ref[...] = jnp.zeros_like(out_ref)
    for r in range(RANKS):
        total = 0.0
        base = BASES[r] // 8 * 8
        for group, usable in ((slab, None), (jnp.clip(side, 0, last), valid)):
            tile = group * RANKS + r
            w = weight_z(z - offsets_ref[0, tile])
            if usable is not None:
                w = jnp.where(usable, w, 0.0)
            total = total + w * table_ref[pl.ds(PAD + base - offsets_ref[1, tile], STRIP), :]
        out_ref[base : base + STRIP, :] += total
    out_ref[...] = 1.0 / jnp.maximum(out_ref[...] * cols_ref[0:1, :], FLOOR)


def join_kernel(frames_ref, recip_ref, out_ref, held):
    done = 0
    for r in range(RANKS):
        base = BASES[r]
        for k in range(0, FRAME, 16):
            n = min(16, FRAME - k)
            part = frames_ref[r, k : k + n, :].astype(jnp.float32)
            row = base + k
            old = max(0, min(n, done - row))
            if old:
                held[row : row + old, :] += part[:old]
            if old < n:
                held[row + old : row + n, :] = part[old:]
        done = base + FRAME
    for k in range(0, MY, 16):
        n = min(16, MY - k)
        out_ref[0, k : k + n, :] = (held[k : k + n, :] * recip_ref[k : k + n, :]).astype(jnp.bfloat16)


def cost(flops, moved):
    return pl.CostEstimate(flops=flops, bytes_accessed=moved, transcendentals=0)


def exchange(block, turn):
    slabs = lax.axis_size("slab")
    pairs = [(i, i + 1) for i in range(1 - turn, slabs - 1, 2)]
    return lax.ppermute(block, "slab", pairs + [(b, a) for a, b in pairs])


def shards(tiles, offsets, fracs):
    call = functools.partial(pl.pallas_call)
    params = pltpu.CompilerParams(vmem_limit_bytes=32 * 2**20)
    wide = pltpu.CompilerParams(vmem_limit_bytes=60 * 2**20)
    shape = jax.ShapeDtypeStruct
    offsets, fracs = offsets.T, fracs.T
    rows, cols = row_table(), column_table()
    rim = shape((RIM, FRAME, TX), jnp.bfloat16)
    work = [pltpu.VMEM((2, SPAN, TX), jnp.float32), pltpu.VMEM((2, FRAME, TX), jnp.float32)]
    frames = shape((RANKS, FRAME, TX), jnp.bfloat16)

    one, two = call(
        rims_kernel,
        out_shape=(rim, rim),
        in_specs=[HBM] * 5,
        out_specs=(VMEM, VMEM),
        scratch_shapes=[
            pltpu.VMEM((2 * RIM + 1, TY, TX), jnp.bfloat16),
            pltpu.SMEM(offsets.shape, jnp.int32),
            pltpu.SMEM(fracs.shape, jnp.int32),
            pltpu.VMEM(rows.shape, jnp.float32),
            pltpu.VMEM(cols.shape, jnp.float32),
            *work,
            pltpu.SemaphoreType.DMA((6,)),
        ],
        compiler_params=wide,
        cost_estimate=cost(10**6, 10**6),
        name="rims",
    )(tiles, offsets, fracs, rows, cols)
    got_one, got_two = exchange(one, 0), exchange(two, 1)
    own, own_rim = call(
        own_kernel,
        out_shape=(frames, shape((2 * RIM, FRAME, TX), jnp.float32)),
        in_specs=[VMEM, SMEM, SMEM, VMEM, VMEM],
        out_specs=(ANY, VMEM),
        scratch_shapes=[
            *work,
            pltpu.VMEM((GROUPZ - 2 * RIM, FRAME, TX), jnp.bfloat16),
            pltpu.SemaphoreType.DMA((GROUPZ - 2 * RIM,)),
        ],
        compiler_params=params,
        cost_estimate=cost(10**7, 3 * 10**6),
        name="own",
    )(tiles, offsets, fracs, rows, cols)
    merged = call(
        merge_kernel,
        out_shape=frames,
        in_specs=[ANY, VMEM, VMEM, VMEM],
        out_specs=ANY,
        scratch_shapes=[pltpu.VMEM((2 * RIM, FRAME, TX), jnp.bfloat16), pltpu.SemaphoreType.DMA((2,))],
        input_output_aliases={0: 0},
        compiler_params=params,
        cost_estimate=cost(3 * 10**6, 2 * 10**6),
        name="merge",
    )(own, own_rim, got_one, got_two)
    received = lax.all_to_all(merged, "tile", split_axis=0, concat_axis=0, tiled=True)
    recip = call(
        weights_kernel,
        out_shape=shape((MYP, TX), jnp.float32),
        in_specs=[SMEM, VMEM, VMEM],
        out_specs=VMEM,
        compiler_params=params,
        cost_estimate=cost(10**7, 4 * 10**6),
        name="weights",
    )(offsets, rows, cols)
    return call(
        join_kernel,
        out_shape=shape((1, MY, TX), jnp.bfloat16),
        in_specs=[VMEM, VMEM],
        out_specs=VMEM,
        scratch_shapes=[pltpu.VMEM((MYP, TX), jnp.float32)],
        compiler_params=params,
        cost_estimate=cost(10**6, 4 * 10**6),
        name="join",
    )(received, recip)


def solution(mesh):
    in_specs = (P(("slab", "tile"), None, None, None), P(), P())
    out_specs = P(("slab", "tile"), None, None)
    return jax.shard_map(shards, mesh=mesh, in_specs=in_specs, out_specs=out_specs, check_vma=False)
```

time: 60.9 us -> 56 us (0.920)
  the two profiles are of different devices: /device:TPU:199 before, /device:TPU:1 now
where the time goes in v2:
time: 56 us; the launch traced here: 55.8 us
  waiting for transfers between devices  28.2 us (50%)
  starting transfers between devices  19.2 us (34%)
  Pallas kernels  8.23 us (15%)
    all_to_all x1, waiting for transfers between devices, shards(): lax.all_to_all(merged, 'tile', split_axis=0, concat_axis=0, tiled=True)  27.4 us
    all_to_all x1, starting transfers between devices, shards(): lax.all_to_all(merged, 'tile', split_axis=0, concat_axis=0, tiled=True)  12.1 us
    ppermute x2, starting transfers between devices, exchange(): return lax.ppermute(block, 'slab', pairs + [(b, a) for a, b in pairs])  7.06 us
    pallas_call x1, Pallas kernels, shards(): call(own_kernel, out_shape=(frames, shape((2 * RIM, FRAME, TX), jnp.float...  2.46 us
    pallas_call x1, Pallas kernels, shards(): call(rims_kernel, out_shape=(rim, rim), in_specs=[HBM] * 5, out_specs=(VM...  2.45 us
    pallas_call x1, Pallas kernels, shards(): call(join_kernel, out_shape=shape((1, MY, TX), jnp.bfloat16), in_specs=[V...  1.26 us
    pallas_call x1, Pallas kernels, shards(): call(weights_kernel, out_shape=shape((MYP, TX), jnp.float32), in_specs=[S...  1.23 us
  transfers between devices with their start and end apart: 3, of which 2 were waited for; matrix products, arithmetic and copies ran while one was open for 0% of the time, Pallas kernels for 7%

profile of v2, /device:TPU:1, one launch (start us, length us, event | category | flops | bytes accessed | tf_op | source)
XLA Modules:
  0.0 55.8 jit_solution(5285184009227794463)
XLA Ops:
  0.0 0.0 copy-start.4
  0.0 0.0 copy-start.1
  0.0 0.0 copy-start
  0.0 0.0 copy-start.3
  0.0 0.0 copy-start.2
  0.0 2.5 %rims.1 = (bf16[3,264,128]{2,1,0:T(8,128)(2,1)}, bf16[3,264,128]{2,1,0:T(8,128)(2,1)}) custom-call(bf16[1,20,256,128]{3,2,1,0:T(8,128)(2,1)} %tiles_ref.3, s32[2,768]{1,0:T(2,128)} %bitcast.2, s32[3,768]{1,0:T(4,128)} %bitcast.5, f32[304,128]{1,0:T(8,128)} %constant.4.clone.table_ref.table_hbm, f32[8,128]{1,0:T(8,128)} %constant.5.clone.cols_ref.cols_hbm), custom_call_target="tpu_custom_call" | custom-call | flops 1000000 | bytes 1000000 | tf_op jit(solution)/shard_map/rims/pallas_call | solution.py:248
  2.5 0.7 %collective-permute-start = (bf16[3,264,128]{2,1,0:T(8,128)(2,1)}, bf16[3,264,128]{2,1,0:T(8,128)(2,1)S(1)}, u32[]{:S(2)}, u32[]{:S(2)}) collective-permute-start(bf16[3,264,128]{2,1,0:T(8,128)(2,1)} %get-tuple-element.11), channel_id=1, source_target_pairs={{16,32},{48,64},{80,96},{112,128},{144,160},{176,192},{208,224},{2... | collective-permute-start | bytes 608264 | tf_op jit(solution)/shard_map/ppermute | solution.py:234
  3.2 6.4 %collective-permute-start.1 = (bf16[3,264,128]{2,1,0:T(8,128)(2,1)}, bf16[3,264,128]{2,1,0:T(8,128)(2,1)S(1)}, u32[]{:S(2)}, u32[]{:S(2)}) collective-permute-start(bf16[3,264,128]{2,1,0:T(8,128)(2,1)} %get-tuple-element.12), channel_id=1, source_target_pairs={{0,16},{32,48},{64,80},{96,112},{128,144},{160,176},{192,208},{224... | collective-permute-start | bytes 608264 | tf_op jit(solution)/shard_map/ppermute | solution.py:234
  9.6 0.0 copy-done.4
  9.6 0.0 copy-done.1
  9.6 0.0 copy-done
  9.6 0.0 copy-done.3
  9.6 0.0 copy-done.2
  9.6 2.5 %own.1 = (bf16[16,264,128]{2,1,0:T(8,128)(2,1)}, f32[6,264,128]{2,1,0:T(8,128)S(1)}) custom-call(bf16[1,20,256,128]{3,2,1,0:T(8,128)(2,1)S(1)} %copy-done, s32[2,768]{1,0:T(2,128)S(1)} %bitcast.3, s32[3,768]{1,0:T(4,128)S(1)} %bitcast.6, f32[304,128]{1,0:T(8,128)S(1)} %copy-done.1, f32[8,128]{1,0:T(8,128)S(1)} %copy-done.4), custom_call_target="tpu_custom_call" | custom-call | flops 10000000 | bytes 3000000 | tf_op jit(solution)/shard_map/own/pallas_call | solution.py:267
  12.1 0.0 collective-permute-done.one_ref
  12.1 0.8 %collective-permute-done.1.two_ref = bf16[3,264,128]{2,1,0:T(8,128)(2,1)S(1)} collective-permute-done((bf16[3,264,128]{2,1,0:T(8,128)(2,1)}, bf16[3,264,128]{2,1,0:T(8,128)(2,1)S(1)}, u32[]{:S(2)}, u32[]{:S(2)}) %collective-permute-start.1) | collective-permute-done | bytes 202784 | tf_op jit(solution)/shard_map/ppermute | solution.py:234
  12.9 0.8 %merge.1 = bf16[16,264,128]{2,1,0:T(8,128)(2,1)} custom-call(bf16[16,264,128]{2,1,0:T(8,128)(2,1)} %get-tuple-element.9.frames_ref, f32[6,264,128]{2,1,0:T(8,128)S(1)} %get-tuple-element.10.rim_ref, bf16[3,264,128]{2,1,0:T(8,128)(2,1)S(1)} %collective-permute-done.one_ref, ...), custom_call_target="tpu_custom_call", output_to_operand_aliasing={{}: (0, {})} | custom-call | flops 3000000 | bytes 2000000 | tf_op jit(solution)/shard_map/merge/pallas_call | solution.py:281
  13.7 12.1 %all-to-all-start = ((bf16[16,264,128]{2,1,0:T(8,128)(2,1)}), bf16[16,264,128]{2,1,0:T(8,128)(2,1)S(1)}, u32[]{:S(2)}, u32[]{:S(2)}) async-start(bf16[16,264,128]{2,1,0:T(8,128)(2,1)} %merge.1), calls=%async_computation | async-start | bytes 2162688 | tf_op jit(solution)/shard_map/all_to_all | solution.py:292
  25.9 1.2 %weights.1.recip_ref = f32[3712,128]{1,0:T(8,128)S(1)} custom-call(s32[2,768]{1,0:T(2,128)S(1)} %bitcast.4, f32[304,128]{1,0:T(8,128)S(1)} %copy-done.1, f32[8,128]{1,0:T(8,128)S(1)} %copy-done.4), custom_call_target="tpu_custom_call" | custom-call | flops 10000000 | bytes 4000000 | tf_op jit(solution)/shard_map/weights/pallas_call | solution.py:293
  27.1 27.4 %all-to-all-done.frames_ref = bf16[16,264,128]{2,1,0:T(8,128)(2,1)S(1)} async-done(((bf16[16,264,128]{2,1,0:T(8,128)(2,1)}), bf16[16,264,128]{2,1,0:T(8,128)(2,1)S(1)}, u32[]{:S(2)}, u32[]{:S(2)}) %all-to-all-start) | async-done | bytes 1081376 | tf_op jit(solution)/shard_map/all_to_all | solution.py:292
  54.5 1.3 %join.1 = bf16[1,3706,128]{2,1,0:T(8,128)(2,1)} custom-call(bf16[16,264,128]{2,1,0:T(8,128)(2,1)S(1)} %all-to-all-done.frames_ref, f32[3712,128]{1,0:T(8,128)S(1)} %weights.1.recip_ref), custom_call_target="tpu_custom_call" | custom-call | flops 1000000 | bytes 4000000 | tf_op jit(solution)/shard_map/join/pallas_call | solution.py:302
Async XLA Ops:
  0.0 9.6 %copy-start.4 = (f32[8,128]{1,0:T(8,128)S(1)}, f32[8,128]{1,0:T(8,128)}, u32[]{:S(2)}) copy-start(f32[8,128]{1,0:T(8,128)} %constant.5.clone.cols_ref.cols_hbm) | copy-start | bytes 12292
  0.0 9.6 %copy-start.1 = (f32[304,128]{1,0:T(8,128)S(1)}, f32[304,128]{1,0:T(8,128)}, u32[]{:S(2)}) copy-start(f32[304,128]{1,0:T(8,128)} %constant.4.clone.table_ref.table_hbm) | copy-start | bytes 466948
  0.0 9.6 %copy-start = (bf16[1,20,256,128]{3,2,1,0:T(8,128)(2,1)S(1)}, bf16[1,20,256,128]{3,2,1,0:T(8,128)(2,1)}, u32[]{:S(2)}) copy-start(bf16[1,20,256,128]{3,2,1,0:T(8,128)(2,1)} %tiles_ref.3) | copy-start | bytes 3932164
  0.0 9.6 %copy-start.3 = (s32[768,3]{0,1:T(4,128)S(1)}, s32[768,3]{0,1:T(4,128)}, u32[]{:S(2)}) copy-start(s32[768,3]{0,1:T(4,128)} %param.7) | copy-start | bytes 27652
  0.0 9.6 %copy-start.2 = (s32[768,2]{0,1:T(2,128)S(1)}, s32[768,2]{0,1:T(2,128)}, u32[]{:S(2)}) copy-start(s32[768,2]{0,1:T(2,128)} %param.6) | copy-start | bytes 18436
  2.5 9.6 %collective-permute-start = (bf16[3,264,128]{2,1,0:T(8,128)(2,1)}, bf16[3,264,128]{2,1,0:T(8,128)(2,1)S(1)}, u32[]{:S(2)}, u32[]{:S(2)}) collective-permute-start(bf16[3,264,128]{2,1,0:T(8,128)(2,1)} %get-tuple-element.11), channel_id=1, source_target_pairs={{16,32},{48,64},{80,96},{112,128},{144,160},{176,192},{208,224},{2... | collective-permute-start | bytes 608264 | tf_op jit(solution)/shard_map/ppermute | solution.py:234
  3.2 9.7 %collective-permute-start.1 = (bf16[3,264,128]{2,1,0:T(8,128)(2,1)}, bf16[3,264,128]{2,1,0:T(8,128)(2,1)S(1)}, u32[]{:S(2)}, u32[]{:S(2)}) collective-permute-start(bf16[3,264,128]{2,1,0:T(8,128)(2,1)} %get-tuple-element.12), channel_id=1, source_target_pairs={{0,16},{32,48},{64,80},{96,112},{128,144},{160,176},{192,208},{224... | collective-permute-start | bytes 608264 | tf_op jit(solution)/shard_map/ppermute | solution.py:234
  13.7 40.8 %all-to-all-start = ((bf16[16,264,128]{2,1,0:T(8,128)(2,1)}), bf16[16,264,128]{2,1,0:T(8,128)(2,1)S(1)}, u32[]{:S(2)}, u32[]{:S(2)}) async-start(bf16[16,264,128]{2,1,0:T(8,128)(2,1)} %merge.1), calls=%async_computation | async-start | bytes 2162688 | tf_op jit(solution)/shard_map/all_to_all | solution.py:292

commit v3 on v2

--- a/solution.py
+++ b/solution.py
@@ -125,10 +125,10 @@
     clear_edges(held)
     for copy in copies:
         copy.wait()
-    slab, _ = spot()
+    slab, rank = spot()
     origin, shift, fz, c0, c1 = tile_terms(offsets_ref, fracs_ref, table_ref, cols_ref, terms)
     for turn, out_ref in enumerate((one_ref, two_ref)):
-        upward = slab % 2 != turn
+        upward = (slab + rank) % 2 != turn
         first = jnp.where(upward, (slab + 1) * GROUPZ, slab * GROUPZ - RIM) - origin
         skipped = jnp.where(upward, TZ - RIM - (RIM + 1), 0)
         for i in range(RIM):
@@ -169,10 +169,10 @@
 
 
 def merge_kernel(frames_ref, rim_ref, one_ref, two_ref, out_ref, sent, sems):
-    slab, _ = spot()
+    slab, rank = spot()
     copies = []
     for turn, source_ref in enumerate((one_ref, two_ref)):
-        side = jnp.where(slab % 2 != turn, 1, 0)
+        side = jnp.where((slab + rank) % 2 != turn, 1, 0)
         for i in range(RIM):
             sent[turn * RIM + i] = (rim_ref[side * RIM + i] + source_ref[i].astype(jnp.float32)).astype(jnp.bfloat16)
         copies.append(
@@ -229,9 +229,9 @@
 
 
 def exchange(block, turn):
-    slabs = lax.axis_size("slab")
-    pairs = [(i, i + 1) for i in range(1 - turn, slabs - 1, 2)]
-    return lax.ppermute(block, "slab", pairs + [(b, a) for a, b in pairs])
+    slabs, ranks = lax.axis_size("slab"), lax.axis_size("tile")
+    pairs = [(s * ranks + r, (s + 1) * ranks + r) for s in range(slabs - 1) for r in range(ranks) if (s + r) % 2 != turn]
+    return lax.ppermute(block, ("slab", "tile"), pairs + [(b, a) for a, b in pairs])
 
 
 def shards(tiles, offsets, fracs):
@@ -247,7 +247,7 @@
 
     one, two = call(
         rims_kernel,
-        out_shape=(rim, rim),
+        out_shape=(pltpu.VMEM(rim.shape, rim.dtype),) * 2,
         in_specs=[HBM] * 5,
         out_specs=(VMEM, VMEM),
         scratch_shapes=[

time: 56 us -> 55.1 us (0.984)
  waiting for transfers between devices: 28.2 us -> 27.4 us
  Pallas kernels: 8.23 us -> 7.55 us
  starting transfers between devices: 19.2 us -> 19.8 us
    all_to_all x1, starting transfers between devices: 12.1 us -> 15.1 us  [shards(): lax.all_to_all(merged, 'tile', split_axis=0, concat_axis=0, tiled=True)]
    ppermute x2, starting transfers between devices: 7.06 us -> 4.62 us  [exchange(): lax.ppermute(block, ('slab', 'tile'), pairs + [(b, a) for a, b in pairs])]
    ppermute x2, waiting for transfers between devices: 0.8 us -> 0.01 us  [exchange(): lax.ppermute(block, ('slab', 'tile'), pairs + [(b, a) for a, b in pairs])]
    pallas_call x1, Pallas kernels: 2.45 us -> 1.77 us  [shards(): call(rims_kernel, out_shape=(pltpu.VMEM(rim.shape, rim.dtype),) * 2, in_s...]
  transfers between devices with their start and end apart: 3 -> 3, of which waited for: 2 -> 1; matrix products, arithmetic and copies ran while one was open for 0% -> 0% of each run, Pallas kernels for 7% -> 7%
where the time goes in v3:
time: 55.1 us; the launch traced here: 54.9 us
  waiting for transfers between devices  27.4 us (50%)
  starting transfers between devices  19.8 us (36%)
  Pallas kernels  7.55 us (14%)
    all_to_all x1, waiting for transfers between devices, shards(): lax.all_to_all(merged, 'tile', split_axis=0, concat_axis=0, tiled=True)  27.4 us
    all_to_all x1, starting transfers between devices, shards(): lax.all_to_all(merged, 'tile', split_axis=0, concat_axis=0, tiled=True)  15.1 us
    ppermute x2, starting transfers between devices, exchange(): lax.ppermute(block, ('slab', 'tile'), pairs + [(b, a) for a, b in pairs])  4.62 us
    pallas_call x1, Pallas kernels, shards(): call(own_kernel, out_shape=(frames, shape((2 * RIM, FRAME, TX), jnp.float...  2.46 us
    pallas_call x1, Pallas kernels, shards(): call(rims_kernel, out_shape=(pltpu.VMEM(rim.shape, rim.dtype),) * 2, in_s...  1.77 us
    pallas_call x1, Pallas kernels, shards(): call(join_kernel, out_shape=shape((1, MY, TX), jnp.bfloat16), in_specs=[V...  1.26 us
    pallas_call x1, Pallas kernels, shards(): call(weights_kernel, out_shape=shape((MYP, TX), jnp.float32), in_specs=[S...  1.23 us
  transfers between devices with their start and end apart: 3, of which 1 were waited for; matrix products, arithmetic and copies ran while one was open for 0% of the time, Pallas kernels for 7%

profile of v3, /device:TPU:1, one launch (start us, length us, event | category | flops | bytes accessed | tf_op | source)
XLA Modules:
  0.0 54.9 jit_solution(10252572240012593899)
XLA Ops:
  0.0 0.0 copy-start.4
  0.0 0.0 copy-start.1
  0.0 0.0 copy-start
  0.0 0.0 copy-start.3
  0.0 0.0 copy-start.2
  0.0 1.8 %rims.1 = (bf16[3,264,128]{2,1,0:T(8,128)(2,1)S(1)}, bf16[3,264,128]{2,1,0:T(8,128)(2,1)S(1)}) custom-call(bf16[1,20,256,128]{3,2,1,0:T(8,128)(2,1)} %tiles_ref.3, s32[2,768]{1,0:T(2,128)} %bitcast.2, s32[3,768]{1,0:T(4,128)} %bitcast.5, f32[304,128]{1,0:T(8,128)} %constant.4.clone.table_ref.table_hbm, f32[8,128]{1,0:T(8,128)} %constant.5.clone.cols_ref.cols_hbm), custom_call_target="tpu_custom_call" | custom-call | flops 1000000 | bytes 1000000 | tf_op jit(solution)/shard_map/rims/pallas_call | solution.py:248
  1.8 3.9 %collective-permute-start = (bf16[3,264,128]{2,1,0:T(8,128)(2,1)S(1)}, bf16[3,264,128]{2,1,0:T(8,128)(2,1)S(1)}, u32[]{:S(2)}, u32[]{:S(2)}) collective-permute-start(bf16[3,264,128]{2,1,0:T(8,128)(2,1)S(1)} %get-tuple-element.11), channel_id=1, source_target_pairs={{1,17},{3,19},{5,21},{7,23},{9,25},{11,27},{13,29},{15,31},{16,32}... | collective-permute-start | bytes 608264 | tf_op jit(solution)/shard_map/ppermute | solution.py:234
  5.8 0.7 %collective-permute-start.1 = (bf16[3,264,128]{2,1,0:T(8,128)(2,1)S(1)}, bf16[3,264,128]{2,1,0:T(8,128)(2,1)S(1)}, u32[]{:S(2)}, u32[]{:S(2)}) collective-permute-start(bf16[3,264,128]{2,1,0:T(8,128)(2,1)S(1)} %get-tuple-element.12), channel_id=1, source_target_pairs={{0,16},{2,18},{4,20},{6,22},{8,24},{10,26},{12,28},{14,30},{17,33}... | collective-permute-start | bytes 608264 | tf_op jit(solution)/shard_map/ppermute | solution.py:234
  6.4 0.0 copy-done.4
  6.5 0.0 copy-done.1
  6.5 0.0 copy-done
  6.5 0.0 copy-done.3
  6.5 0.0 copy-done.2
  6.5 2.5 %own.1 = (bf16[16,264,128]{2,1,0:T(8,128)(2,1)}, f32[6,264,128]{2,1,0:T(8,128)S(1)}) custom-call(bf16[1,20,256,128]{3,2,1,0:T(8,128)(2,1)S(1)} %copy-done, s32[2,768]{1,0:T(2,128)S(1)} %bitcast.3, s32[3,768]{1,0:T(4,128)S(1)} %bitcast.6, f32[304,128]{1,0:T(8,128)S(1)} %copy-done.1, f32[8,128]{1,0:T(8,128)S(1)} %copy-done.4), custom_call_target="tpu_custom_call" | custom-call | flops 10000000 | bytes 3000000 | tf_op jit(solution)/shard_map/own/pallas_call | solution.py:267
  9.0 0.0 collective-permute-done.one_ref
  9.0 0.0 collective-permute-done.1.two_ref
  9.0 0.8 %merge.1 = bf16[16,264,128]{2,1,0:T(8,128)(2,1)} custom-call(bf16[16,264,128]{2,1,0:T(8,128)(2,1)} %get-tuple-element.9.frames_ref, f32[6,264,128]{2,1,0:T(8,128)S(1)} %get-tuple-element.10.rim_ref, bf16[3,264,128]{2,1,0:T(8,128)(2,1)S(1)} %collective-permute-done.one_ref, ...), custom_call_target="tpu_custom_call", output_to_operand_aliasing={{}: (0, {})} | custom-call | flops 3000000 | bytes 2000000 | tf_op jit(solution)/shard_map/merge/pallas_call | solution.py:281
  9.8 15.1 %all-to-all-start = ((bf16[16,264,128]{2,1,0:T(8,128)(2,1)}), bf16[16,264,128]{2,1,0:T(8,128)(2,1)S(1)}, u32[]{:S(2)}, u32[]{:S(2)}) async-start(bf16[16,264,128]{2,1,0:T(8,128)(2,1)} %merge.1), calls=%async_computation | async-start | bytes 2162688 | tf_op jit(solution)/shard_map/all_to_all | solution.py:292
  25.0 1.2 %weights.1.recip_ref = f32[3712,128]{1,0:T(8,128)S(1)} custom-call(s32[2,768]{1,0:T(2,128)S(1)} %bitcast.4, f32[304,128]{1,0:T(8,128)S(1)} %copy-done.1, f32[8,128]{1,0:T(8,128)S(1)} %copy-done.4), custom_call_target="tpu_custom_call" | custom-call | flops 10000000 | bytes 4000000 | tf_op jit(solution)/shard_map/weights/pallas_call | solution.py:293
  26.2 27.4 %all-to-all-done.frames_ref = bf16[16,264,128]{2,1,0:T(8,128)(2,1)S(1)} async-done(((bf16[16,264,128]{2,1,0:T(8,128)(2,1)}), bf16[16,264,128]{2,1,0:T(8,128)(2,1)S(1)}, u32[]{:S(2)}, u32[]{:S(2)}) %all-to-all-start) | async-done | bytes 1081376 | tf_op jit(solution)/shard_map/all_to_all | solution.py:292
  53.6 1.3 %join.1 = bf16[1,3706,128]{2,1,0:T(8,128)(2,1)} custom-call(bf16[16,264,128]{2,1,0:T(8,128)(2,1)S(1)} %all-to-all-done.frames_ref, f32[3712,128]{1,0:T(8,128)S(1)} %weights.1.recip_ref), custom_call_target="tpu_custom_call" | custom-call | flops 1000000 | bytes 4000000 | tf_op jit(solution)/shard_map/join/pallas_call | solution.py:302
Async XLA Ops:
  0.0 6.4 %copy-start.4 = (f32[8,128]{1,0:T(8,128)S(1)}, f32[8,128]{1,0:T(8,128)}, u32[]{:S(2)}) copy-start(f32[8,128]{1,0:T(8,128)} %constant.5.clone.cols_ref.cols_hbm) | copy-start | bytes 12292
  0.0 6.5 %copy-start.1 = (f32[304,128]{1,0:T(8,128)S(1)}, f32[304,128]{1,0:T(8,128)}, u32[]{:S(2)}) copy-start(f32[304,128]{1,0:T(8,128)} %constant.4.clone.table_ref.table_hbm) | copy-start | bytes 466948
  0.0 6.5 %copy-start = (bf16[1,20,256,128]{3,2,1,0:T(8,128)(2,1)S(1)}, bf16[1,20,256,128]{3,2,1,0:T(8,128)(2,1)}, u32[]{:S(2)}) copy-start(bf16[1,20,256,128]{3,2,1,0:T(8,128)(2,1)} %tiles_ref.3) | copy-start | bytes 3932164
  0.0 6.5 %copy-start.3 = (s32[768,3]{0,1:T(4,128)S(1)}, s32[768,3]{0,1:T(4,128)}, u32[]{:S(2)}) copy-start(s32[768,3]{0,1:T(4,128)} %param.7) | copy-start | bytes 27652
  0.0 6.5 %copy-start.2 = (s32[768,2]{0,1:T(2,128)S(1)}, s32[768,2]{0,1:T(2,128)}, u32[]{:S(2)}) copy-start(s32[768,2]{0,1:T(2,128)} %param.6) | copy-start | bytes 18436
  1.8 7.2 %collective-permute-start = (bf16[3,264,128]{2,1,0:T(8,128)(2,1)S(1)}, bf16[3,264,128]{2,1,0:T(8,128)(2,1)S(1)}, u32[]{:S(2)}, u32[]{:S(2)}) collective-permute-start(bf16[3,264,128]{2,1,0:T(8,128)(2,1)S(1)} %get-tuple-element.11), channel_id=1, source_target_pairs={{1,17},{3,19},{5,21},{7,23},{9,25},{11,27},{13,29},{15,31},{16,32}... | collective-permute-start | bytes 608264 | tf_op jit(solution)/shard_map/ppermute | solution.py:234
  5.8 3.2 %collective-permute-start.1 = (bf16[3,264,128]{2,1,0:T(8,128)(2,1)S(1)}, bf16[3,264,128]{2,1,0:T(8,128)(2,1)S(1)}, u32[]{:S(2)}, u32[]{:S(2)}) collective-permute-start(bf16[3,264,128]{2,1,0:T(8,128)(2,1)S(1)} %get-tuple-element.12), channel_id=1, source_target_pairs={{0,16},{2,18},{4,20},{6,22},{8,24},{10,26},{12,28},{14,30},{17,33}... | collective-permute-start | bytes 608264 | tf_op jit(solution)/shard_map/ppermute | solution.py:234
  9.8 43.8 %all-to-all-start = ((bf16[16,264,128]{2,1,0:T(8,128)(2,1)}), bf16[16,264,128]{2,1,0:T(8,128)(2,1)S(1)}, u32[]{:S(2)}, u32[]{:S(2)}) async-start(bf16[16,264,128]{2,1,0:T(8,128)(2,1)} %merge.1), calls=%async_computation | async-start | bytes 2162688 | tf_op jit(solution)/shard_map/all_to_all | solution.py:292
